TPU v7x, 32 devices: a whole 2x2x4 slice. The times are simulated.
32 devices in a mesh: vis: 4 (over y, core), row: 4 (over z), col: 2 (over x).
Axes of the slice: x: 2, y: 2, z: 4, core: 2. Of those that a mesh axis runs over, the one named last changes fastest.
Arguments:
- partials: bfloat16 [4, 2, 512, 512], P('vis', None, 'row', 'col'), may hold values from -6 to 6
- coverage: int32 [4, 4, 4], P('vis', 'row', 'col'), may hold values from 0 to 1, as said below
- conv_one: float32 [32, 3, 3], replicated, may hold values from -2 to 2
- bias_one: float32 [32], replicated, may hold values from -3 to 3
- conv_two: bfloat16 [3, 3, 32, 32], replicated, may hold values from -0.375 to 0.375
- bias_two: float32 [32], replicated, may hold values from -3 to 3
Outputs:
- features: bfloat16 [32, 256, 256], P(None, ('vis', 'row', 'col'))
Inputs may be any that keep to these rules, and one draw needn't show every extreme that they name: `coverage`: 0 or 1; blocks near the grid's centre are touched by more groups than those near its corners.
All inputs are finite; a program needn't handle non-finite values.
Results may differ from a plain program's by a relative error of at most 0.014.
Values may be sent and summed in bfloat16 or wider, within the bound.
No kernel may reach another device: no remote copies, remote signals or barrier semaphores. Data moves between devices by JAX's collectives and lax.ppermute only.
A program may use at most 64 MiB of HBM per device.

v0:
```python
import math

import jax
import jax.numpy as jnp
import numpy as np
from jax import lax
from jax.experimental import pallas as pl
from jax.experimental.pallas import tpu as pltpu
from jax.sharding import PartitionSpec as P

BLK = 128
ALL = ("vis", "row", "col")
DIRECT_BYTES = 4 * 2**20
HALO = 2
TILE = 8
LANES = 128


def with_halo(cells, sides, width):
    for axis, dim in sides:
        count = lax.axis_size(axis)
        ends = count - 1
        head = lax.slice_in_dim(cells, 0, width, axis=dim)
        tail = lax.slice_in_dim(cells, cells.shape[dim] - width, cells.shape[dim], axis=dim)
        cells = jnp.concatenate(
            [
                lax.ppermute(tail, axis, [(i, (i + 1) % count) for i in range(ends)]),
                cells,
                lax.ppermute(head, axis, [((i + 1) % count, i) for i in range(ends)]),
            ],
            axis=dim,
        )
    return cells


def phase_table(numer, denom):
    angle = numer.astype(jnp.float32) * (2.0 * math.pi / denom)
    return (jnp.cos(angle), jnp.sin(angle))


def partial_transform(real_part, imag_part, block_of, keep_imag):
    batch = real_part.shape[0]
    count_blocks = real_part.shape[1]
    block_len = real_part.shape[2]
    length = count_blocks * block_len
    highest = lax.Precision.HIGHEST
    outer = jnp.arange(count_blocks, dtype=jnp.int32)
    inner = jnp.arange(block_len, dtype=jnp.int32)
    cos_one, sin_one = phase_table(block_of[:, None] * outer[None, :] % count_blocks, count_blocks)
    mid_re = jnp.einsum("lpt,px->lxt", real_part, cos_one, precision=highest) - jnp.einsum(
        "lpt,px->lxt", imag_part, sin_one, precision=highest
    )
    mid_im = jnp.einsum("lpt,px->lxt", real_part, sin_one, precision=highest) + jnp.einsum(
        "lpt,px->lxt", imag_part, cos_one, precision=highest
    )
    cos_two, sin_two = phase_table(outer[:, None] * inner[None, :] % length, length)
    parity = (1 - 2 * (outer % 2)).astype(jnp.float32)[:, None]
    cos_two = cos_two * parity
    sin_two = sin_two * parity
    turn_re = mid_re * cos_two - mid_im * sin_two
    turn_im = mid_re * sin_two + mid_im * cos_two
    kept = jnp.arange(block_len // 2, dtype=jnp.int32)
    picked = (kept + 3 * block_len // 4) % block_len
    cos_three, sin_three = phase_table(inner[:, None] * picked[None, :] % block_len, block_len)
    out_re = jnp.einsum("lxt,tj->ljx", turn_re, cos_three, precision=highest) - jnp.einsum(
        "lxt,tj->ljx", turn_im, sin_three, precision=highest
    )
    out_re = out_re.reshape(batch, length // 2)
    if keep_imag:
        out_im = jnp.einsum("lxt,tj->ljx", turn_re, sin_three, precision=highest) + jnp.einsum(
            "lxt,tj->ljx", turn_im, cos_three, precision=highest
        )
        return (out_re, out_im.reshape(batch, length // 2))
    return (out_re, out_re)


def first_layer(extended, conv_one, bias_one, count_rows):
    width = extended.shape[1]
    padded = jnp.pad(extended, ((0, 0), (1, 1)))
    summed = (
        jnp.zeros((conv_one.shape[0], count_rows, width), jnp.float32) + bias_one[:, None, None]
    )
    for shift_b in range(3):
        for shift_a in range(3):
            summed = (
                summed
                + conv_one[:, shift_b, shift_a][:, None, None]
                * padded[None, shift_b : shift_b + count_rows, shift_a : shift_a + width]
            )
    return jnp.maximum(summed, 0.0)


def second_layer(hidden_ext, conv_two, bias_two, count_rows):
    width = hidden_ext.shape[2]
    padded = jnp.pad(hidden_ext, ((0, 0), (0, 0), (1, 1)))
    summed = jnp.zeros((conv_two.shape[2], count_rows, width), jnp.float32)
    for shift_b in range(3):
        for shift_a in range(3):
            summed = summed + jnp.einsum(
                "kj,jba->kba",
                conv_two[shift_b, shift_a],
                padded[:, shift_b : shift_b + count_rows, shift_a : shift_a + width],
                preferred_element_type=jnp.float32,
            )
    return (summed + bias_two[:, None, None]).astype(jnp.bfloat16)


def staged(partials, coverage, conv_one, bias_one, conv_two, bias_two):
    count_vis = lax.axis_size("vis")
    count_row = lax.axis_size("row")
    count_col = lax.axis_size("col")
    grid_len = partials.shape[3] * count_col
    cover = coverage[0]
    block_rows = cover.shape[0]
    block_cols = cover.shape[1]
    spread = jnp.broadcast_to(cover[:, None, :, None], (block_rows, BLK, block_cols, BLK))
    spread = spread.reshape(block_rows * BLK, block_cols * BLK)
    count_blocks = count_vis * count_row
    row_block = grid_len // count_blocks
    row_share = row_block // count_col
    masked = partials[0] * spread.astype(jnp.bfloat16)[None]
    reduced = lax.psum_scatter(
        masked.astype(jnp.float32).astype(jnp.bfloat16), "vis", scatter_dimension=1, tiled=True
    ).astype(jnp.float32)
    grid_rows = lax.all_to_all(
        reduced.astype(jnp.bfloat16), "col", split_axis=1, concat_axis=2, tiled=True
    ).astype(reduced.dtype)
    natural = jnp.arange(count_blocks, dtype=jnp.int32)
    shaped = grid_rows.reshape(2, row_share, count_blocks, row_block)
    first_re, first_im = partial_transform(shaped[0], shaped[1], natural, True)
    stacked = jnp.stack([first_re, first_im])
    moved = lax.all_to_all(
        lax.all_to_all(
            stacked.astype(jnp.bfloat16), ("vis", "row"), split_axis=2, concat_axis=1, tiled=True
        ),
        "col",
        split_axis=2,
        concat_axis=1,
        tiled=True,
    ).astype(stacked.dtype)
    img_rows = moved.shape[2]
    arranged = moved.reshape(2, count_col, count_blocks, row_share, img_rows)
    arranged = arranged.transpose(0, 4, 2, 1, 3).reshape(2, img_rows, count_blocks, row_block)
    owners = natural % count_row * count_vis + natural // count_row
    image, unused = partial_transform(arranged[0], arranged[1], owners, False)
    image = image * (1.0 / grid_len)
    extended = with_halo(image.astype(jnp.bfloat16), ((("vis", "row", "col"), 0),), 1).astype(
        image.dtype
    )
    hidden = first_layer(extended, conv_one, bias_one, img_rows).astype(jnp.bfloat16)
    hidden_ext = with_halo(hidden, ((("vis", "row", "col"), 1),), 1)
    return second_layer(hidden_ext, conv_two, bias_two, img_rows)


def grid_tables(length, count_row, count_col):
    image_len = length // 2
    place = np.arange(length)[:, None] - length // 2
    pixel = np.arange(image_len)[None, :] - image_len // 2
    angle = (place * pixel % length) * (2.0 * math.pi / length)
    cos, sin = np.cos(angle), np.sin(angle)
    padded = np.pad(np.stack([cos.T, sin.T]), ((0, 0), (HALO, TILE - HALO), (0, 0)))
    first = padded.reshape(2 * (image_len + TILE), count_col, length // count_col).transpose(1, 0, 2)
    rows = length // count_row
    second = np.stack([cos.reshape(count_row, rows, image_len), -sin.reshape(count_row, rows, image_len)], axis=1)
    second = second.reshape(2 * length, image_len) / length
    return first.astype(jnp.bfloat16), second.astype(jnp.bfloat16)


def share_kernel(cover_in, parts_in, first_all, out, cover, parts, first, sems):
    get_cover = pltpu.make_async_copy(cover_in, cover, sems.at[0])
    get_parts = pltpu.make_async_copy(parts_in, parts, sems.at[1])
    get_first = pltpu.make_async_copy(first_all.at[lax.axis_index("col")], first, sems.at[2])
    for copy in (get_cover, get_parts, get_first):
        copy.start()
    count_rows = parts.shape[2]
    get_cover.wait()
    get_parts.wait()
    components = []
    for component in range(2):
        strips = []
        for i in range(cover.shape[1]):
            cells = []
            for j in range(cover.shape[2]):
                block = parts[0, component, i * BLK : (i + 1) * BLK, j * BLK : (j + 1) * BLK]
                level = jnp.full(block.shape, cover[0, i, j].astype(jnp.float32)).astype(jnp.bfloat16)
                cells.append(block * level)
            strips.append(jnp.concatenate(cells, axis=1))
        components.append(jnp.concatenate(strips, axis=0))
    grid = jnp.concatenate(components, axis=0)
    upper = lax.broadcasted_iota(jnp.int32, (TILE, LANES), 0) < TILE // 2
    devices = out.shape[0]
    tall = first.shape[0] // 2
    get_first.wait()
    turned = lax.dot_general(first[...], grid, (((1,), (1,)), ((), ())), preferred_element_type=jnp.float32)
    mid_re = turned[:tall, :count_rows] - turned[tall:, count_rows:]
    mid_im = turned[tall:, :count_rows] + turned[:tall, count_rows:]
    for device in range(devices):
        here = slice(TILE * device, TILE * (device + 1))
        below = slice(TILE * (device + 1), TILE * (device + 2))
        middle = jnp.where(upper, mid_re[below], pltpu.roll(mid_im[below], TILE // 2, 0))
        out[device] = jnp.concatenate([mid_re[here], middle, mid_im[here]], axis=0).astype(out.dtype)


def own_place():
    place, count = 0, 1
    for axis in ALL:
        place = place * lax.axis_size(axis) + lax.axis_index(axis)
        count = count * lax.axis_size(axis)
    return place, count - 1


def four_times(values):
    return jnp.concatenate([values] * 4, axis=1)


def weights_kernel(
    one_in, bias_in, two_in, bias_two_in, table_in, weights_one, weights_two, bias_rows, table, one, bias, two, bias_two, sems
):
    fetch = [
        pltpu.make_async_copy(one_in, one, sems.at[0]),
        pltpu.make_async_copy(bias_in, bias, sems.at[1]),
        pltpu.make_async_copy(two_in, two, sems.at[2]),
        pltpu.make_async_copy(bias_two_in, bias_two, sems.at[3]),
    ]
    get_table = pltpu.make_async_copy(table_in, table, sems.at[4])
    for copy in (*fetch, get_table):
        copy.start()
    for copy in fetch:
        copy.wait()
    channels = one.shape[2]
    rows = TILE + 2
    per_tile = LANES // channels
    lanes = -(-rows * channels // LANES) * LANES
    image_row = lax.broadcasted_iota(jnp.int32, (16, lanes), 0)
    hidden_row = lax.broadcasted_iota(jnp.int32, (16, lanes), 1) // channels
    place, last = own_place()
    held = (hidden_row >= jnp.where(place == 0, 1, 0)) & (hidden_row < jnp.where(place == last, rows - 1, rows))
    high, low = [], []
    for tap in range(3):
        band = jnp.zeros((16, lanes), jnp.float32)
        for shift in range(3):
            line = jnp.concatenate([four_times(one[shift, tap : tap + 1])] * (lanes // LANES), axis=1)
            band = jnp.where(held & (image_row - hidden_row == shift), line, band)
        high.append(band.astype(jnp.bfloat16).astype(jnp.float32))
        low.append(band - high[-1])
    line = jnp.concatenate([four_times(bias[...])] * (lanes // LANES), axis=1)
    with_bias = high[0]
    for piece in range(3):
        rounded = line.astype(jnp.bfloat16).astype(jnp.float32)
        with_bias = jnp.where(held & (image_row == 12 + piece), rounded, with_bias)
        line = line - rounded
    stacked = jnp.concatenate([with_bias, *high[1:], *high, *low], axis=0)
    weights_one[...] = stacked.T[: weights_one.shape[0]].astype(jnp.bfloat16)
    row = lax.broadcasted_iota(jnp.int32, bias_rows.shape, 0) // TILE
    lane = lax.broadcasted_iota(jnp.int32, bias_rows.shape, 1)
    line = jnp.where(row == lane, four_times(bias_two[...]), 0.0)
    bias_rows[...] = jnp.broadcast_to(jnp.sum(line, axis=1, keepdims=True), bias_rows.shape)
    lines = [[four_times(two[shift, tap].astype(jnp.float32)) for shift in range(3)] for tap in range(3)]
    row = lax.broadcasted_iota(jnp.int32, (TILE, LANES), 0)
    lane = lax.broadcasted_iota(jnp.int32, (TILE, LANES), 1) // channels
    zero = jnp.zeros((TILE, LANES), jnp.float32)
    for tile in range(-(-3 * rows // per_tile)):
        taps = sorted({(tile * per_tile + g) // rows for g in range(per_tile)} & {0, 1, 2})
        masks = []
        for tap in taps:
            hidden_row = tile * per_tile + lane - tap * rows
            inside = (hidden_row >= 0) & (hidden_row < rows)
            masks += [(tap, shift, inside & (hidden_row - row == shift)) for shift in range(3)]
        width = min(LANES, weights_two.shape[1] - tile * LANES)
        for channel in range(0, channels, 2):
            pair = []
            for k in (channel, channel + 1):
                values = zero
                for tap, shift, mask in masks:
                    values = jnp.where(mask, lines[tap][shift][k : k + 1], values)
                pair.append(values)
            block = jnp.concatenate(pair, axis=0).astype(jnp.bfloat16)
            weights_two[TILE * channel : TILE * (channel + 2), tile * LANES : tile * LANES + width] = block[:, :width]
    get_table.wait()


def shifted(values, width):
    lane = lax.broadcasted_iota(jnp.int32, values.shape, 1)
    zero = jnp.zeros_like(values)
    before = jnp.where(lane == 0, zero, pltpu.roll(values, 1, 1))
    after = jnp.where(lane == width - 1, zero, pltpu.roll(values, width - 1, 1))
    return before, values, after


def layers_kernel(shares, weights_one, weights_two, bias_rows, table, out, staged, sems):
    width = out.shape[2]
    vis, row, col = (lax.axis_size(axis) for axis in ALL)
    upper = lax.broadcasted_iota(jnp.int32, (TILE, LANES), 0) < TILE // 2
    above, below = [], []
    for r in range(row):
        senders = [(v * row + r) * col + c for v in range(vis) for c in range(col)]
        total = shares[senders[0]].astype(jnp.float32)
        for sender in senders[1:]:
            total = total + shares[sender].astype(jnp.float32)
        middle = total[TILE : 2 * TILE]
        above += [total[:TILE], total[2 * TILE :]]
        below += [jnp.where(upper, middle, 0.0), jnp.where(upper, pltpu.roll(middle, TILE // 2, 0), 0.0)]
    turned = jnp.concatenate([jnp.concatenate(above, axis=1), jnp.concatenate(below, axis=1)], axis=0)
    high = turned.astype(jnp.bfloat16)
    low = (turned - high.astype(jnp.float32)).astype(jnp.bfloat16)
    image = jnp.dot(jnp.concatenate([high, low], axis=0), table[...], preferred_element_type=jnp.float32)
    image = image[: 2 * TILE] + image[2 * TILE :]
    columns = jnp.concatenate(shifted(image, width), axis=0)
    high = columns.astype(jnp.bfloat16).astype(jnp.float32)
    low = columns - high
    row = lax.broadcasted_iota(jnp.int32, (48, width), 0)
    with_ones = jnp.where((row >= 12) & (row < 15), 1.0, high)
    stacked = jnp.concatenate([with_ones, low, high], axis=0).astype(jnp.bfloat16)
    hidden = jnp.dot(weights_one[...], stacked, preferred_element_type=jnp.float32)
    hidden = jnp.maximum(hidden, 0.0).astype(jnp.bfloat16)
    stacked = jnp.concatenate(shifted(hidden, width), axis=0)
    half = out.shape[0] // 2
    copies = []
    for part in range(2):
        rows = pl.ds(part * half * TILE, half * TILE)
        features = jnp.dot(weights_two[rows], stacked, preferred_element_type=jnp.float32)
        features = features + jnp.concatenate([bias_rows[rows]] * (width // LANES), axis=1)
        channels_of = pl.ds(part * half, half)
        staged[channels_of] = features.reshape(half, TILE, width).astype(out.dtype)
        copies.append(pltpu.make_async_copy(staged.at[channels_of], out.at[channels_of], sems.at[part]))
        copies[-1].start()
    for copy in copies:
        copy.wait()


def in_hbm(*arrays):
    return [pltpu.with_memory_space_constraint(array, pltpu.HBM) for array in arrays]


def direct(partials, coverage, conv_one, bias_one, conv_two, bias_two):
    count_row, count_col = lax.axis_size("row"), lax.axis_size("col")
    devices = lax.axis_size("vis") * count_row * count_col
    length = partials.shape[3] * count_col
    image_len = length // 2
    channels = conv_two.shape[2]
    first, second = grid_tables(length, count_row, count_col)
    vmem, hbm = pl.BlockSpec(memory_space=pltpu.VMEM), pl.BlockSpec(memory_space=pltpu.HBM)
    limit = pltpu.CompilerParams(vmem_limit_bytes=16 * 2**20)
    share = (devices, 2 * (TILE + 2 * HALO), LANES)
    shares = pl.pallas_call(
        share_kernel,
        out_shape=jax.ShapeDtypeStruct(share, jnp.bfloat16),
        in_specs=[hbm] * 3,
        out_specs=vmem,
        scratch_shapes=[
            pltpu.SMEM(coverage.shape, jnp.int32),
            pltpu.VMEM(partials.shape, jnp.bfloat16),
            pltpu.VMEM(first.shape[1:], jnp.bfloat16),
            pltpu.SemaphoreType.DMA((3,)),
        ],
        compiler_params=limit,
        name="shares",
    )(*in_hbm(coverage, partials, jnp.asarray(first)))
    arrived = lax.all_to_all(shares, ALL, split_axis=0, concat_axis=0, tiled=True)
    rows = TILE + 2
    weights = pl.pallas_call(
        weights_kernel,
        out_shape=[
            jax.ShapeDtypeStruct((rows * channels, 3 * 48), jnp.bfloat16),
            jax.ShapeDtypeStruct((TILE * channels, 3 * rows * channels), jnp.bfloat16),
            jax.ShapeDtypeStruct((TILE * channels, LANES), jnp.float32),
            jax.ShapeDtypeStruct(second.shape, jnp.bfloat16),
        ],
        in_specs=[hbm] * 5,
        out_specs=[vmem] * 4,
        scratch_shapes=[
            pltpu.VMEM((3, 3, channels), jnp.float32),
            pltpu.VMEM((1, channels), jnp.float32),
            pltpu.VMEM(conv_two.shape, jnp.bfloat16),
            pltpu.VMEM((1, channels), jnp.float32),
            pltpu.SemaphoreType.DMA((5,)),
        ],
        compiler_params=limit,
        name="weights",
    )(*in_hbm(conv_one.transpose(1, 2, 0), bias_one[None], conv_two, bias_two[None], jnp.asarray(second)))
    return pl.pallas_call(
        layers_kernel,
        out_shape=jax.ShapeDtypeStruct((channels, TILE, image_len), jnp.bfloat16),
        in_specs=[vmem] * 5,
        out_specs=hbm,
        scratch_shapes=[
            pltpu.VMEM((channels, TILE, image_len), jnp.bfloat16),
            pltpu.SemaphoreType.DMA((2,)),
        ],
        compiler_params=limit,
        name="layers",
    )(arrived, *weights)


def local(partials, coverage, conv_one, bias_one, conv_two, bias_two):
    count_col = lax.axis_size("col")
    devices = lax.axis_size("vis") * lax.axis_size("row") * count_col
    image_len = partials.shape[3] * count_col // 2
    sent = devices * (TILE + 2 * HALO) * image_len * 2
    fits = partials.shape[2] == LANES and image_len == devices * TILE and conv_two.shape[2] * 4 == LANES and image_len == 2 * LANES and sent <= DIRECT_BYTES
    plan = direct if fits else staged
    return plan(partials, coverage, conv_one, bias_one, conv_two, bias_two)


def solution(mesh):
    placed = (P("vis", None, "row", "col"), P("vis", "row", "col"), P(), P(), P(), P())
    return jax.shard_map(
        local,
        mesh=mesh,
        in_specs=placed,
        out_specs=P(None, ALL, None),
        check_vma=False,
    )
```

profile of v0, /device:TPU:0, one launch (start us, length us, event | category | flops | bytes accessed | tf_op | source)
XLA Modules:
  0.0 19.4 jit_solution(5857660343971836952)
XLA Ops:
  0.0 2.0 %shares.1 = bf16[32,24,128]{2,1,0:T(8,128)(2,1)} custom-call(s32[1,1,2]{2,1,0:T(1,128)} %cover_in.1, bf16[1,2,128,256]{3,2,1,0:T(8,128)(2,1)} %parts_in.1, bf16[2,528,256]{2,1,0:T(8,128)(2,1)} %constant.4.clone.first_all), custom_call_target="tpu_custom_call" | custom-call | tf_op jit(solution)/shard_map/shares/pallas_call | solution.py:345
  2.0 7.3 %all-to-all-start = ((bf16[32,24,128]{2,1,0:T(8,128)(2,1)}), bf16[32,24,128]{2,1,0:T(8,128)(2,1)S(1)}, u32[]{:S(2)}, u32[]{:S(2)}) async-start(bf16[32,24,128]{2,1,0:T(8,128)(2,1)} %shares.1), calls=%async_computation | async-start | bytes 393216 | tf_op jit(solution)/shard_map/all_to_all | solution.py:359
  9.3 1.5 %weights.1 = (bf16[320,144]{1,0:T(8,128)(2,1)S(1)}, bf16[256,960]{1,0:T(8,128)(2,1)S(1)}, f32[256,128]{1,0:T(8,128)S(1)}, bf16[1024,256]{1,0:T(8,128)(2,1)S(1)}) custom-call(f32[3,3,32]{2,1,0:T(4,128)} %bitcast.3, f32[1,32]{1,0:T(1,128)} %bitcast.4, bf16[3,3,32,32]{3,2,1,0:T(8,128)(2,1)} %two_in.1, f32[1,32]{1,0:T(1,128)} %bitcast.5, ...), custom_call_target="tpu_custom_call" | custom-call | tf_op jit(solution)/shard_map/weights/pallas_call | solution.py:361
  10.8 7.0 %all-to-all-done.shares = bf16[32,24,128]{2,1,0:T(8,128)(2,1)S(1)} async-done(((bf16[32,24,128]{2,1,0:T(8,128)(2,1)}), bf16[32,24,128]{2,1,0:T(8,128)(2,1)S(1)}, u32[]{:S(2)}, u32[]{:S(2)}) %all-to-all-start) | async-done | bytes 196640 | tf_op jit(solution)/shard_map/all_to_all | solution.py:359
  17.8 1.5 %layers.1 = bf16[32,8,256]{2,1,0:T(8,128)(2,1)} custom-call(bf16[32,24,128]{2,1,0:T(8,128)(2,1)S(1)} %all-to-all-done.shares, bf16[320,144]{1,0:T(8,128)(2,1)S(1)} %get-tuple-element.9.weights_one, bf16[256,960]{1,0:T(8,128)(2,1)S(1)} %get-tuple-element.10.weights_two, f32[256,128]{1,0:T(8,128)S(1)} %get-tuple-element.11.bias_rows, ...), custom_call_target="tpu_custom_call" | custom-call | tf_op jit(solution)/shard_map/layers/pallas_call | solution.py:381
Async XLA Ops:
  2.0 15.9 %all-to-all-start = ((bf16[32,24,128]{2,1,0:T(8,128)(2,1)}), bf16[32,24,128]{2,1,0:T(8,128)(2,1)S(1)}, u32[]{:S(2)}, u32[]{:S(2)}) async-start(bf16[32,24,128]{2,1,0:T(8,128)(2,1)} %shares.1), calls=%async_computation | async-start | bytes 393216 | tf_op jit(solution)/shard_map/all_to_all | solution.py:359
where the time goes:
time: 19.6 us; the launch traced here: 19.4 us
  starting transfers between devices  7.3 us (37%)
  waiting for transfers between devices  7.01 us (36%)
  Pallas kernels  5.04 us (26%)
    all_to_all x1, starting transfers between devices, direct(): lax.all_to_all(shares, ALL, split_axis=0, concat_axis=0, tiled=True)  7.3 us
    all_to_all x1, waiting for transfers between devices, direct(): lax.all_to_all(shares, ALL, split_axis=0, concat_axis=0, tiled=True)  7.01 us
    pallas_call x1, Pallas kernels, direct(): pl.pallas_call(share_kernel, out_shape=jax.ShapeDtypeStruct(share, jnp.bf...  1.98 us
    pallas_call x1, Pallas kernels, direct(): pl.pallas_call(weights_kernel, out_shape=[jax.ShapeDtypeStruct((rows * ch...  1.53 us
    pallas_call x1, Pallas kernels, direct(): pl.pallas_call(layers_kernel, out_shape=jax.ShapeDtypeStruct((channels, T...  1.53 us
  transfers between devices with their start and end apart: 1, of which 1 were waited for; matrix products, arithmetic and copies ran while one was open for 0% of the time, Pallas kernels for 8%

commit v1 on v0

--- a/solution.py
+++ b/solution.py
@@ -166,7 +166,7 @@
     return first.astype(jnp.bfloat16), second.astype(jnp.bfloat16)
 
 
-def share_kernel(cover_in, parts_in, first_all, out, cover, parts, first, sems):
+def share_kernel(cover_in, parts_in, first_all, out, cover, parts, first, cut, sems, sent):
     get_cover = pltpu.make_async_copy(cover_in, cover, sems.at[0])
     get_parts = pltpu.make_async_copy(parts_in, parts, sems.at[1])
     get_first = pltpu.make_async_copy(first_all.at[lax.axis_index("col")], first, sems.at[2])
@@ -188,17 +188,28 @@
         components.append(jnp.concatenate(strips, axis=0))
     grid = jnp.concatenate(components, axis=0)
     upper = lax.broadcasted_iota(jnp.int32, (TILE, LANES), 0) < TILE // 2
-    devices = out.shape[0]
+    devices = cut.shape[0]
     tall = first.shape[0] // 2
+    group = devices // sent.shape[0]
     get_first.wait()
-    turned = lax.dot_general(first[...], grid, (((1,), (1,)), ((), ())), preferred_element_type=jnp.float32)
-    mid_re = turned[:tall, :count_rows] - turned[tall:, count_rows:]
-    mid_im = turned[tall:, :count_rows] + turned[:tall, count_rows:]
-    for device in range(devices):
-        here = slice(TILE * device, TILE * (device + 1))
-        below = slice(TILE * (device + 1), TILE * (device + 2))
-        middle = jnp.where(upper, mid_re[below], pltpu.roll(mid_im[below], TILE // 2, 0))
-        out[device] = jnp.concatenate([mid_re[here], middle, mid_im[here]], axis=0).astype(out.dtype)
+    copies = []
+    for start in range(0, devices, group):
+        rows = slice(TILE * start, TILE * (start + group + 1))
+        table = jnp.concatenate([first[rows], first[tall + rows.start : tall + rows.stop]], axis=0)
+        turned = lax.dot_general(table, grid, (((1,), (1,)), ((), ())), preferred_element_type=jnp.float32)
+        half = turned.shape[0] // 2
+        mid_re = turned[:half, :count_rows] - turned[half:, count_rows:]
+        mid_im = turned[half:, :count_rows] + turned[:half, count_rows:]
+        for k in range(group):
+            here = slice(TILE * k, TILE * (k + 1))
+            below = slice(TILE * (k + 1), TILE * (k + 2))
+            middle = jnp.where(upper, mid_re[below], pltpu.roll(mid_im[below], TILE // 2, 0))
+            cut[start + k] = jnp.concatenate([mid_re[here], middle, mid_im[here]], axis=0).astype(cut.dtype)
+        part = pl.ds(start, group)
+        copies.append(pltpu.make_async_copy(cut.at[part], out.at[part], sent.at[start // group]))
+        copies[-1].start()
+    for copy in copies:
+        copy.wait()
 
 
 def own_place():
@@ -279,12 +290,12 @@
     get_table.wait()
 
 
-def shifted(values, width):
-    lane = lax.broadcasted_iota(jnp.int32, values.shape, 1)
-    zero = jnp.zeros_like(values)
-    before = jnp.where(lane == 0, zero, pltpu.roll(values, 1, 1))
-    after = jnp.where(lane == width - 1, zero, pltpu.roll(values, width - 1, 1))
-    return before, values, after
+def shifted(values, by):
+    if by == 0:
+        return values
+    width = values.shape[1]
+    lane = lax.broadcasted_iota(jnp.int32, values.shape, 1) + by
+    return jnp.where((lane >= 0) & (lane < width), pltpu.roll(values, -by % width, 1), 0.0)
 
 
 def layers_kernel(shares, weights_one, weights_two, bias_rows, table, out, staged, sems):
@@ -305,15 +316,21 @@
     low = (turned - high.astype(jnp.float32)).astype(jnp.bfloat16)
     image = jnp.dot(jnp.concatenate([high, low], axis=0), table[...], preferred_element_type=jnp.float32)
     image = image[: 2 * TILE] + image[2 * TILE :]
-    columns = jnp.concatenate(shifted(image, width), axis=0)
-    high = columns.astype(jnp.bfloat16).astype(jnp.float32)
-    low = columns - high
+    moved = [shifted(image, by) for by in range(-2, 3)]
     row = lax.broadcasted_iota(jnp.int32, (48, width), 0)
-    with_ones = jnp.where((row >= 12) & (row < 15), 1.0, high)
-    stacked = jnp.concatenate([with_ones, low, high], axis=0).astype(jnp.bfloat16)
-    hidden = jnp.dot(weights_one[...], stacked, preferred_element_type=jnp.float32)
+    lane = lax.broadcasted_iota(jnp.int32, (48, width), 1)
+    stacked = []
+    for by in (-1, 0, 1):
+        columns = jnp.concatenate(moved[by + 1 : by + 4], axis=0)
+        high = columns.astype(jnp.bfloat16).astype(jnp.float32)
+        low = columns - high
+        with_ones = jnp.where((row >= 12) & (row < 15), 1.0, high)
+        inside = (lane + by >= 0) & (lane + by < width)
+        pieces = [jnp.where(inside, piece, 0.0) for piece in (with_ones, low, high)]
+        stacked.append(jnp.concatenate(pieces, axis=0).astype(jnp.bfloat16))
+    hidden = jnp.dot(weights_one[...], jnp.concatenate(stacked, axis=1), preferred_element_type=jnp.float32)
     hidden = jnp.maximum(hidden, 0.0).astype(jnp.bfloat16)
-    stacked = jnp.concatenate(shifted(hidden, width), axis=0)
+    stacked = jnp.concatenate([hidden[:, i * width : (i + 1) * width] for i in range(3)], axis=0)
     half = out.shape[0] // 2
     copies = []
     for part in range(2):
@@ -346,12 +363,14 @@
         share_kernel,
         out_shape=jax.ShapeDtypeStruct(share, jnp.bfloat16),
         in_specs=[hbm] * 3,
-        out_specs=vmem,
+        out_specs=hbm,
         scratch_shapes=[
             pltpu.SMEM(coverage.shape, jnp.int32),
             pltpu.VMEM(partials.shape, jnp.bfloat16),
             pltpu.VMEM(first.shape[1:], jnp.bfloat16),
+            pltpu.VMEM(share, jnp.bfloat16),
             pltpu.SemaphoreType.DMA((3,)),
+            pltpu.SemaphoreType.DMA((math.gcd(devices, 2),)),
         ],
         compiler_params=limit,
         name="shares",

time: 19.6 us -> 19.6 us (level)
  no operation moved by 1% of the time
where the time goes in v1:
time: 19.6 us; the launch traced here: 19.4 us
  starting transfers between devices  7.3 us (37%)
  waiting for transfers between devices  7.01 us (36%)
  Pallas kernels  5.1 us (26%)
    all_to_all x1, starting transfers between devices, direct(): lax.all_to_all(shares, ALL, split_axis=0, concat_axis=0, tiled=True)  7.3 us
    all_to_all x1, waiting for transfers between devices, direct(): lax.all_to_all(shares, ALL, split_axis=0, concat_axis=0, tiled=True)  7.01 us
    pallas_call x1, Pallas kernels, direct(): pl.pallas_call(share_kernel, out_shape=jax.ShapeDtypeStruct(share, jnp.bf...  2 us
    pallas_call x1, Pallas kernels, direct(): pl.pallas_call(layers_kernel, out_shape=jax.ShapeDtypeStruct((channels, T...  1.57 us
    pallas_call x1, Pallas kernels, direct(): pl.pallas_call(weights_kernel, out_shape=[jax.ShapeDtypeStruct((rows * ch...  1.53 us
  transfers between devices with their start and end apart: 1, of which 1 were waited for; matrix products, arithmetic and copies ran while one was open for 0% of the time, Pallas kernels for 8%

profile of v1, /device:TPU:0, one launch (start us, length us, event | category | flops | bytes accessed | tf_op | source)
XLA Modules:
  0.0 19.4 jit_solution(755939611945282224)
XLA Ops:
  0.0 2.0 %shares.1 = bf16[32,24,128]{2,1,0:T(8,128)(2,1)} custom-call(s32[1,1,2]{2,1,0:T(1,128)} %cover_in.1, bf16[1,2,128,256]{3,2,1,0:T(8,128)(2,1)} %parts_in.1, bf16[2,528,256]{2,1,0:T(8,128)(2,1)} %constant.4.clone.first_all), custom_call_target="tpu_custom_call" | custom-call | tf_op jit(solution)/shard_map/shares/pallas_call | solution.py:362
  2.0 7.3 %all-to-all-start = ((bf16[32,24,128]{2,1,0:T(8,128)(2,1)}), bf16[32,24,128]{2,1,0:T(8,128)(2,1)S(1)}, u32[]{:S(2)}, u32[]{:S(2)}) async-start(bf16[32,24,128]{2,1,0:T(8,128)(2,1)} %shares.1), calls=%async_computation | async-start | bytes 393216 | tf_op jit(solution)/shard_map/all_to_all | solution.py:378
  9.3 1.5 %weights.1 = (bf16[320,144]{1,0:T(8,128)(2,1)S(1)}, bf16[256,960]{1,0:T(8,128)(2,1)S(1)}, f32[256,128]{1,0:T(8,128)S(1)}, bf16[1024,256]{1,0:T(8,128)(2,1)S(1)}) custom-call(f32[3,3,32]{2,1,0:T(4,128)} %bitcast.3, f32[1,32]{1,0:T(1,128)} %bitcast.4, bf16[3,3,32,32]{3,2,1,0:T(8,128)(2,1)} %two_in.1, f32[1,32]{1,0:T(1,128)} %bitcast.5, ...), custom_call_target="tpu_custom_call" | custom-call | tf_op jit(solution)/shard_map/weights/pallas_call | solution.py:380
  10.9 7.0 %all-to-all-done.shares = bf16[32,24,128]{2,1,0:T(8,128)(2,1)S(1)} async-done(((bf16[32,24,128]{2,1,0:T(8,128)(2,1)}), bf16[32,24,128]{2,1,0:T(8,128)(2,1)S(1)}, u32[]{:S(2)}, u32[]{:S(2)}) %all-to-all-start) | async-done | bytes 196640 | tf_op jit(solution)/shard_map/all_to_all | solution.py:378
  17.9 1.6 %layers.1 = bf16[32,8,256]{2,1,0:T(8,128)(2,1)} custom-call(bf16[32,24,128]{2,1,0:T(8,128)(2,1)S(1)} %all-to-all-done.shares, bf16[320,144]{1,0:T(8,128)(2,1)S(1)} %get-tuple-element.9.weights_one, bf16[256,960]{1,0:T(8,128)(2,1)S(1)} %get-tuple-element.10.weights_two, f32[256,128]{1,0:T(8,128)S(1)} %get-tuple-element.11.bias_rows, ...), custom_call_target="tpu_custom_call" | custom-call | tf_op jit(solution)/shard_map/layers/pallas_call | solution.py:400
Async XLA Ops:
  2.0 15.9 %all-to-all-start = ((bf16[32,24,128]{2,1,0:T(8,128)(2,1)}), bf16[32,24,128]{2,1,0:T(8,128)(2,1)S(1)}, u32[]{:S(2)}, u32[]{:S(2)}) async-start(bf16[32,24,128]{2,1,0:T(8,128)(2,1)} %shares.1), calls=%async_computation | async-start | bytes 393216 | tf_op jit(solution)/shard_map/all_to_all | solution.py:378

commit v2 on v0

--- a/solution.py
+++ b/solution.py
@@ -290,20 +290,22 @@
 def layers_kernel(shares, weights_one, weights_two, bias_rows, table, out, staged, sems):
     width = out.shape[2]
     vis, row, col = (lax.axis_size(axis) for axis in ALL)
-    upper = lax.broadcasted_iota(jnp.int32, (TILE, LANES), 0) < TILE // 2
-    above, below = [], []
+    upper = lax.broadcasted_iota(jnp.int32, (TILE, 2 * LANES), 0) < TILE // 2
+    depth = 2 * LANES
+    image = jnp.zeros((4 * TILE, width), jnp.float32)
     for r in range(row):
         senders = [(v * row + r) * col + c for v in range(vis) for c in range(col)]
         total = shares[senders[0]].astype(jnp.float32)
         for sender in senders[1:]:
             total = total + shares[sender].astype(jnp.float32)
         middle = total[TILE : 2 * TILE]
-        above += [total[:TILE], total[2 * TILE :]]
-        below += [jnp.where(upper, middle, 0.0), jnp.where(upper, pltpu.roll(middle, TILE // 2, 0), 0.0)]
-    turned = jnp.concatenate([jnp.concatenate(above, axis=1), jnp.concatenate(below, axis=1)], axis=0)
-    high = turned.astype(jnp.bfloat16)
-    low = (turned - high.astype(jnp.float32)).astype(jnp.bfloat16)
-    image = jnp.dot(jnp.concatenate([high, low], axis=0), table[...], preferred_element_type=jnp.float32)
+        above = jnp.concatenate([total[:TILE], total[2 * TILE :]], axis=1)
+        below = jnp.concatenate([middle, pltpu.roll(middle, TILE // 2, 0)], axis=1)
+        turned = jnp.concatenate([above, jnp.where(upper, below, 0.0)], axis=0)
+        high = turned.astype(jnp.bfloat16)
+        low = (turned - high.astype(jnp.float32)).astype(jnp.bfloat16)
+        block = table[r * depth : (r + 1) * depth]
+        image = image + jnp.dot(jnp.concatenate([high, low], axis=0), block, preferred_element_type=jnp.float32)
     image = image[: 2 * TILE] + image[2 * TILE :]
     columns = jnp.concatenate(shifted(image, width), axis=0)
     high = columns.astype(jnp.bfloat16).astype(jnp.float32)

time: 19.6 us -> 19.6 us (level)
  no operation moved by 1% of the time
where the time goes in v2:
time: 19.6 us; the launch traced here: 19.4 us
  starting transfers between devices  7.3 us (37%)
  waiting for transfers between devices  7.01 us (36%)
  Pallas kernels  5.04 us (26%)
    all_to_all x1, starting transfers between devices, direct(): lax.all_to_all(shares, ALL, split_axis=0, concat_axis=0, tiled=True)  7.3 us
    all_to_all x1, waiting for transfers between devices, direct(): lax.all_to_all(shares, ALL, split_axis=0, concat_axis=0, tiled=True)  7.01 us
    pallas_call x1, Pallas kernels, direct(): pl.pallas_call(share_kernel, out_shape=jax.ShapeDtypeStruct(share, jnp.bf...  1.98 us
    pallas_call x1, Pallas kernels, direct(): pl.pallas_call(weights_kernel, out_shape=[jax.ShapeDtypeStruct((rows * ch...  1.53 us
    pallas_call x1, Pallas kernels, direct(): pl.pallas_call(layers_kernel, out_shape=jax.ShapeDtypeStruct((channels, T...  1.53 us
  transfers between devices with their start and end apart: 1, of which 1 were waited for; matrix products, arithmetic and copies ran while one was open for 0% of the time, Pallas kernels for 8%

profile of v2, /device:TPU:0, one launch (start us, length us, event | category | flops | bytes accessed | tf_op | source)
XLA Modules:
  0.0 19.4 jit_solution(11345431880505257801)
XLA Ops:
  0.0 2.0 %shares.1 = bf16[32,24,128]{2,1,0:T(8,128)(2,1)} custom-call(s32[1,1,2]{2,1,0:T(1,128)} %cover_in.1, bf16[1,2,128,256]{3,2,1,0:T(8,128)(2,1)} %parts_in.1, bf16[2,528,256]{2,1,0:T(8,128)(2,1)} %constant.4.clone.first_all), custom_call_target="tpu_custom_call" | custom-call | tf_op jit(solution)/shard_map/shares/pallas_call | solution.py:347
  2.0 7.3 %all-to-all-start = ((bf16[32,24,128]{2,1,0:T(8,128)(2,1)}), bf16[32,24,128]{2,1,0:T(8,128)(2,1)S(1)}, u32[]{:S(2)}, u32[]{:S(2)}) async-start(bf16[32,24,128]{2,1,0:T(8,128)(2,1)} %shares.1), calls=%async_computation | async-start | bytes 393216 | tf_op jit(solution)/shard_map/all_to_all | solution.py:361
  9.3 1.5 %weights.1 = (bf16[320,144]{1,0:T(8,128)(2,1)S(1)}, bf16[256,960]{1,0:T(8,128)(2,1)S(1)}, f32[256,128]{1,0:T(8,128)S(1)}, bf16[1024,256]{1,0:T(8,128)(2,1)S(1)}) custom-call(f32[3,3,32]{2,1,0:T(4,128)} %bitcast.3, f32[1,32]{1,0:T(1,128)} %bitcast.4, bf16[3,3,32,32]{3,2,1,0:T(8,128)(2,1)} %two_in.1, f32[1,32]{1,0:T(1,128)} %bitcast.5, ...), custom_call_target="tpu_custom_call" | custom-call | tf_op jit(solution)/shard_map/weights/pallas_call | solution.py:363
  10.8 7.0 %all-to-all-done.shares = bf16[32,24,128]{2,1,0:T(8,128)(2,1)S(1)} async-done(((bf16[32,24,128]{2,1,0:T(8,128)(2,1)}), bf16[32,24,128]{2,1,0:T(8,128)(2,1)S(1)}, u32[]{:S(2)}, u32[]{:S(2)}) %all-to-all-start) | async-done | bytes 196640 | tf_op jit(solution)/shard_map/all_to_all | solution.py:361
  17.8 1.5 %layers.1 = bf16[32,8,256]{2,1,0:T(8,128)(2,1)} custom-call(bf16[32,24,128]{2,1,0:T(8,128)(2,1)S(1)} %all-to-all-done.shares, bf16[320,144]{1,0:T(8,128)(2,1)S(1)} %get-tuple-element.9.weights_one, bf16[256,960]{1,0:T(8,128)(2,1)S(1)} %get-tuple-element.10.weights_two, f32[256,128]{1,0:T(8,128)S(1)} %get-tuple-element.11.bias_rows, ...), custom_call_target="tpu_custom_call" | custom-call | tf_op jit(solution)/shard_map/layers/pallas_call | solution.py:383
Async XLA Ops:
  2.0 15.9 %all-to-all-start = ((bf16[32,24,128]{2,1,0:T(8,128)(2,1)}), bf16[32,24,128]{2,1,0:T(8,128)(2,1)S(1)}, u32[]{:S(2)}, u32[]{:S(2)}) async-start(bf16[32,24,128]{2,1,0:T(8,128)(2,1)} %shares.1), calls=%async_computation | async-start | bytes 393216 | tf_op jit(solution)/shard_map/all_to_all | solution.py:361

commit v3 on v2

--- a/solution.py
+++ b/solution.py
@@ -316,14 +316,14 @@
     hidden = jnp.dot(weights_one[...], stacked, preferred_element_type=jnp.float32)
     hidden = jnp.maximum(hidden, 0.0).astype(jnp.bfloat16)
     stacked = jnp.concatenate(shifted(hidden, width), axis=0)
+    features = jnp.dot(weights_two[...], stacked, preferred_element_type=jnp.float32)
     half = out.shape[0] // 2
     copies = []
     for part in range(2):
-        rows = pl.ds(part * half * TILE, half * TILE)
-        features = jnp.dot(weights_two[rows], stacked, preferred_element_type=jnp.float32)
-        features = features + jnp.concatenate([bias_rows[rows]] * (width // LANES), axis=1)
         channels_of = pl.ds(part * half, half)
-        staged[channels_of] = features.reshape(half, TILE, width).astype(out.dtype)
+        rows = slice(part * half * TILE, (part + 1) * half * TILE)
+        biased = features[rows] + jnp.concatenate([bias_rows[rows]] * (width // LANES), axis=1)
+        staged[channels_of] = biased.reshape(half, TILE, width).astype(out.dtype)
         copies.append(pltpu.make_async_copy(staged.at[channels_of], out.at[channels_of], sems.at[part]))
         copies[-1].start()
     for copy in copies:

time: 19.6 us -> 19.7 us (level)
  no operation moved by 1% of the time
where the time goes in v3:
time: 19.7 us; the launch traced here: 19.5 us
  starting transfers between devices  7.3 us (37%)
  waiting for transfers between devices  7.01 us (36%)
  Pallas kernels  5.12 us (26%)
    all_to_all x1, starting transfers between devices, direct(): lax.all_to_all(shares, ALL, split_axis=0, concat_axis=0, tiled=True)  7.3 us
    all_to_all x1, waiting for transfers between devices, direct(): lax.all_to_all(shares, ALL, split_axis=0, concat_axis=0, tiled=True)  7.01 us
    pallas_call x1, Pallas kernels, direct(): pl.pallas_call(share_kernel, out_shape=jax.ShapeDtypeStruct(share, jnp.bf...  1.98 us
    pallas_call x1, Pallas kernels, direct(): pl.pallas_call(layers_kernel, out_shape=jax.ShapeDtypeStruct((channels, T...  1.61 us
    pallas_call x1, Pallas kernels, direct(): pl.pallas_call(weights_kernel, out_shape=[jax.ShapeDtypeStruct((rows * ch...  1.53 us
  transfers between devices with their start and end apart: 1, of which 1 were waited for; matrix products, arithmetic and copies ran while one was open for 0% of the time, Pallas kernels for 8%

profile of v3, /device:TPU:0, one launch (start us, length us, event | category | flops | bytes accessed | tf_op | source)
XLA Modules:
  0.0 19.5 jit_solution(18227964212168718941)
XLA Ops:
  0.0 2.0 %shares.1 = bf16[32,24,128]{2,1,0:T(8,128)(2,1)} custom-call(s32[1,1,2]{2,1,0:T(1,128)} %cover_in.1, bf16[1,2,128,256]{3,2,1,0:T(8,128)(2,1)} %parts_in.1, bf16[2,528,256]{2,1,0:T(8,128)(2,1)} %constant.4.clone.first_all), custom_call_target="tpu_custom_call" | custom-call | tf_op jit(solution)/shard_map/shares/pallas_call | solution.py:347
  2.0 7.3 %all-to-all-start = ((bf16[32,24,128]{2,1,0:T(8,128)(2,1)}), bf16[32,24,128]{2,1,0:T(8,128)(2,1)S(1)}, u32[]{:S(2)}, u32[]{:S(2)}) async-start(bf16[32,24,128]{2,1,0:T(8,128)(2,1)} %shares.1), calls=%async_computation | async-start | bytes 393216 | tf_op jit(solution)/shard_map/all_to_all | solution.py:361
  9.3 1.5 %weights.1 = (bf16[320,144]{1,0:T(8,128)(2,1)S(1)}, bf16[256,960]{1,0:T(8,128)(2,1)S(1)}, f32[256,128]{1,0:T(8,128)S(1)}, bf16[1024,256]{1,0:T(8,128)(2,1)S(1)}) custom-call(f32[3,3,32]{2,1,0:T(4,128)} %bitcast.3, f32[1,32]{1,0:T(1,128)} %bitcast.4, bf16[3,3,32,32]{3,2,1,0:T(8,128)(2,1)} %two_in.1, f32[1,32]{1,0:T(1,128)} %bitcast.5, ...), custom_call_target="tpu_custom_call" | custom-call | tf_op jit(solution)/shard_map/weights/pallas_call | solution.py:363
  10.8 7.0 %all-to-all-done.shares = bf16[32,24,128]{2,1,0:T(8,128)(2,1)S(1)} async-done(((bf16[32,24,128]{2,1,0:T(8,128)(2,1)}), bf16[32,24,128]{2,1,0:T(8,128)(2,1)S(1)}, u32[]{:S(2)}, u32[]{:S(2)}) %all-to-all-start) | async-done | bytes 196640 | tf_op jit(solution)/shard_map/all_to_all | solution.py:361
  17.8 1.6 %layers.1 = bf16[32,8,256]{2,1,0:T(8,128)(2,1)} custom-call(bf16[32,24,128]{2,1,0:T(8,128)(2,1)S(1)} %all-to-all-done.shares, bf16[320,144]{1,0:T(8,128)(2,1)S(1)} %get-tuple-element.9.weights_one, bf16[256,960]{1,0:T(8,128)(2,1)S(1)} %get-tuple-element.10.weights_two, f32[256,128]{1,0:T(8,128)S(1)} %get-tuple-element.11.bias_rows, ...), custom_call_target="tpu_custom_call" | custom-call | tf_op jit(solution)/shard_map/layers/pallas_call | solution.py:383
Async XLA Ops:
  2.0 15.9 %all-to-all-start = ((bf16[32,24,128]{2,1,0:T(8,128)(2,1)}), bf16[32,24,128]{2,1,0:T(8,128)(2,1)S(1)}, u32[]{:S(2)}, u32[]{:S(2)}) async-start(bf16[32,24,128]{2,1,0:T(8,128)(2,1)} %shares.1), calls=%async_computation | async-start | bytes 393216 | tf_op jit(solution)/shard_map/all_to_all | solution.py:361

commit v4 on v2

--- a/solution.py
+++ b/solution.py
@@ -186,12 +186,12 @@
                 cells.append(block * level)
             strips.append(jnp.concatenate(cells, axis=1))
         components.append(jnp.concatenate(strips, axis=0))
-    grid = jnp.concatenate(components, axis=0)
+    grid = jnp.concatenate(components, axis=0).T
     upper = lax.broadcasted_iota(jnp.int32, (TILE, LANES), 0) < TILE // 2
     devices = out.shape[0]
     tall = first.shape[0] // 2
     get_first.wait()
-    turned = lax.dot_general(first[...], grid, (((1,), (1,)), ((), ())), preferred_element_type=jnp.float32)
+    turned = jnp.dot(first[...], grid, preferred_element_type=jnp.float32)
     mid_re = turned[:tall, :count_rows] - turned[tall:, count_rows:]
     mid_im = turned[tall:, :count_rows] + turned[:tall, count_rows:]
     for device in range(devices):

time: 19.6 us -> 19.6 us (level)
  no operation moved by 1% of the time
where the time goes in v4:
time: 19.6 us; the launch traced here: 19.4 us
  starting transfers between devices  7.3 us (37%)
  waiting for transfers between devices  7.01 us (36%)
  Pallas kernels  5.04 us (26%)
    all_to_all x1, starting transfers between devices, direct(): lax.all_to_all(shares, ALL, split_axis=0, concat_axis=0, tiled=True)  7.3 us
    all_to_all x1, waiting for transfers between devices, direct(): lax.all_to_all(shares, ALL, split_axis=0, concat_axis=0, tiled=True)  7.01 us
    pallas_call x1, Pallas kernels, direct(): pl.pallas_call(share_kernel, out_shape=jax.ShapeDtypeStruct(share, jnp.bf...  1.98 us
    pallas_call x1, Pallas kernels, direct(): pl.pallas_call(weights_kernel, out_shape=[jax.ShapeDtypeStruct((rows * ch...  1.53 us
    pallas_call x1, Pallas kernels, direct(): pl.pallas_call(layers_kernel, out_shape=jax.ShapeDtypeStruct((channels, T...  1.53 us
  transfers between devices with their start and end apart: 1, of which 1 were waited for; matrix products, arithmetic and copies ran while one was open for 0% of the time, Pallas kernels for 8%

profile of v4, /device:TPU:0, one launch (start us, length us, event | category | flops | bytes accessed | tf_op | source)
XLA Modules:
  0.0 19.4 jit_solution(11345431880505257801)
XLA Ops:
  0.0 2.0 %shares.1 = bf16[32,24,128]{2,1,0:T(8,128)(2,1)} custom-call(s32[1,1,2]{2,1,0:T(1,128)} %cover_in.1, bf16[1,2,128,256]{3,2,1,0:T(8,128)(2,1)} %parts_in.1, bf16[2,528,256]{2,1,0:T(8,128)(2,1)} %constant.4.clone.first_all), custom_call_target="tpu_custom_call" | custom-call | tf_op jit(solution)/shard_map/shares/pallas_call | solution.py:347
  2.0 7.3 %all-to-all-start = ((bf16[32,24,128]{2,1,0:T(8,128)(2,1)}), bf16[32,24,128]{2,1,0:T(8,128)(2,1)S(1)}, u32[]{:S(2)}, u32[]{:S(2)}) async-start(bf16[32,24,128]{2,1,0:T(8,128)(2,1)} %shares.1), calls=%async_computation | async-start | bytes 393216 | tf_op jit(solution)/shard_map/all_to_all | solution.py:361
  9.3 1.5 %weights.1 = (bf16[320,144]{1,0:T(8,128)(2,1)S(1)}, bf16[256,960]{1,0:T(8,128)(2,1)S(1)}, f32[256,128]{1,0:T(8,128)S(1)}, bf16[1024,256]{1,0:T(8,128)(2,1)S(1)}) custom-call(f32[3,3,32]{2,1,0:T(4,128)} %bitcast.3, f32[1,32]{1,0:T(1,128)} %bitcast.4, bf16[3,3,32,32]{3,2,1,0:T(8,128)(2,1)} %two_in.1, f32[1,32]{1,0:T(1,128)} %bitcast.5, ...), custom_call_target="tpu_custom_call" | custom-call | tf_op jit(solution)/shard_map/weights/pallas_call | solution.py:363
  10.8 7.0 %all-to-all-done.shares = bf16[32,24,128]{2,1,0:T(8,128)(2,1)S(1)} async-done(((bf16[32,24,128]{2,1,0:T(8,128)(2,1)}), bf16[32,24,128]{2,1,0:T(8,128)(2,1)S(1)}, u32[]{:S(2)}, u32[]{:S(2)}) %all-to-all-start) | async-done | bytes 196640 | tf_op jit(solution)/shard_map/all_to_all | solution.py:361
  17.8 1.5 %layers.1 = bf16[32,8,256]{2,1,0:T(8,128)(2,1)} custom-call(bf16[32,24,128]{2,1,0:T(8,128)(2,1)S(1)} %all-to-all-done.shares, bf16[320,144]{1,0:T(8,128)(2,1)S(1)} %get-tuple-element.9.weights_one, bf16[256,960]{1,0:T(8,128)(2,1)S(1)} %get-tuple-element.10.weights_two, f32[256,128]{1,0:T(8,128)S(1)} %get-tuple-element.11.bias_rows, ...), custom_call_target="tpu_custom_call" | custom-call | tf_op jit(solution)/shard_map/layers/pallas_call | solution.py:383
Async XLA Ops:
  2.0 15.9 %all-to-all-start = ((bf16[32,24,128]{2,1,0:T(8,128)(2,1)}), bf16[32,24,128]{2,1,0:T(8,128)(2,1)S(1)}, u32[]{:S(2)}, u32[]{:S(2)}) async-start(bf16[32,24,128]{2,1,0:T(8,128)(2,1)} %shares.1), calls=%async_computation | async-start | bytes 393216 | tf_op jit(solution)/shard_map/all_to_all | solution.py:361

commit v5 on v0

--- a/solution.py
+++ b/solution.py
@@ -1,3 +1,4 @@
+import functools
 import math
 
 import jax
@@ -152,26 +153,51 @@
     return second_layer(hidden_ext, conv_two, bias_two, img_rows)
 
 
-def grid_tables(length, count_row, count_col):
+def grid_table(length):
     image_len = length // 2
     place = np.arange(length)[:, None] - length // 2
     pixel = np.arange(image_len)[None, :] - image_len // 2
     angle = (place * pixel % length) * (2.0 * math.pi / length)
-    cos, sin = np.cos(angle), np.sin(angle)
-    padded = np.pad(np.stack([cos.T, sin.T]), ((0, 0), (HALO, TILE - HALO), (0, 0)))
-    first = padded.reshape(2 * (image_len + TILE), count_col, length // count_col).transpose(1, 0, 2)
-    rows = length // count_row
-    second = np.stack([cos.reshape(count_row, rows, image_len), -sin.reshape(count_row, rows, image_len)], axis=1)
-    second = second.reshape(2 * length, image_len) / length
-    return first.astype(jnp.bfloat16), second.astype(jnp.bfloat16)
-
-
-def share_kernel(cover_in, parts_in, first_all, out, cover, parts, first, sems):
+    cos, sin = (wave.reshape(-1, LANES, image_len) for wave in (np.cos(angle), np.sin(angle)))
+    return (np.stack([cos, -sin], axis=1).reshape(2 * length, image_len) / length).astype(jnp.bfloat16)
+
+
+def phases(numer, length):
+    turn = numer & (length - 1)
+    turn = jnp.where(turn >= length // 2, turn - length, turn)
+    angle = turn.astype(jnp.float32) * (2.0 * math.pi / length)
+    return jnp.cos(angle), jnp.sin(angle)
+
+
+def make_first(first, length):
+    tall, cols = first.shape[0] // 2, first.shape[1]
+    image_len = tall - TILE
+    blocks = -(-tall // (TILE * TILE)) * TILE
+    start = lax.axis_index("col") * cols - length // 2
+    row = lax.broadcasted_iota(jnp.int32, (blocks, cols), 0) * TILE - HALO - image_len // 2
+    cos_far, sin_far = phases(row * (start + lax.broadcasted_iota(jnp.int32, (blocks, cols), 1)), length)
+    row = lax.broadcasted_iota(jnp.int32, (TILE, cols), 0)
+    cos_near, sin_near = phases(row * (start + lax.broadcasted_iota(jnp.int32, (TILE, cols), 1)), length)
+    cosines, sines = [], []
+    for k in range(tall // TILE):
+        cos_at, sin_at = cos_far[k : k + 1], sin_far[k : k + 1]
+        cos = cos_at * cos_near - sin_at * sin_near
+        sin = sin_at * cos_near + cos_at * sin_near
+        pixel = row + (TILE * k - HALO)
+        if k == 0 or k == tall // TILE - 1:
+            inside = (pixel >= 0) & (pixel < image_len)
+            cos, sin = jnp.where(inside, cos, 0.0), jnp.where(inside, sin, 0.0)
+        cosines.append(cos)
+        sines.append(sin)
+    first[...] = jnp.concatenate(cosines + sines, axis=0).astype(first.dtype)
+
+
+def share_kernel(length, cover_in, parts_in, out, cover, parts, first, sems):
     get_cover = pltpu.make_async_copy(cover_in, cover, sems.at[0])
     get_parts = pltpu.make_async_copy(parts_in, parts, sems.at[1])
-    get_first = pltpu.make_async_copy(first_all.at[lax.axis_index("col")], first, sems.at[2])
-    for copy in (get_cover, get_parts, get_first):
+    for copy in (get_parts, get_cover):
         copy.start()
+    make_first(first, length)
     count_rows = parts.shape[2]
     get_cover.wait()
     get_parts.wait()
@@ -190,7 +216,6 @@
     upper = lax.broadcasted_iota(jnp.int32, (TILE, LANES), 0) < TILE // 2
     devices = out.shape[0]
     tall = first.shape[0] // 2
-    get_first.wait()
     turned = lax.dot_general(first[...], grid, (((1,), (1,)), ((), ())), preferred_element_type=jnp.float32)
     mid_re = turned[:tall, :count_rows] - turned[tall:, count_rows:]
     mid_im = turned[tall:, :count_rows] + turned[:tall, count_rows:]
@@ -338,24 +363,24 @@
     length = partials.shape[3] * count_col
     image_len = length // 2
     channels = conv_two.shape[2]
-    first, second = grid_tables(length, count_row, count_col)
+    second = grid_table(length)
     vmem, hbm = pl.BlockSpec(memory_space=pltpu.VMEM), pl.BlockSpec(memory_space=pltpu.HBM)
     limit = pltpu.CompilerParams(vmem_limit_bytes=16 * 2**20)
     share = (devices, 2 * (TILE + 2 * HALO), LANES)
     shares = pl.pallas_call(
-        share_kernel,
+        functools.partial(share_kernel, length),
         out_shape=jax.ShapeDtypeStruct(share, jnp.bfloat16),
-        in_specs=[hbm] * 3,
+        in_specs=[hbm] * 2,
         out_specs=vmem,
         scratch_shapes=[
             pltpu.SMEM(coverage.shape, jnp.int32),
             pltpu.VMEM(partials.shape, jnp.bfloat16),
-            pltpu.VMEM(first.shape[1:], jnp.bfloat16),
-            pltpu.SemaphoreType.DMA((3,)),
+            pltpu.VMEM((2 * (image_len + TILE), partials.shape[3]), jnp.bfloat16),
+            pltpu.SemaphoreType.DMA((2,)),
         ],
         compiler_params=limit,
         name="shares",
-    )(*in_hbm(coverage, partials, jnp.asarray(first)))
+    )(*in_hbm(coverage, partials))
     arrived = lax.all_to_all(shares, ALL, split_axis=0, concat_axis=0, tiled=True)
     rows = TILE + 2
     weights = pl.pallas_call(

time: 19.6 us -> 19.5 us (level)
  no operation moved by 1% of the time
where the time goes in v5:
time: 19.5 us; the launch traced here: 19.3 us
  starting transfers between devices  7.3 us (37%)
  waiting for transfers between devices  7.01 us (36%)
  Pallas kernels  4.92 us (25%)
    all_to_all x1, starting transfers between devices, direct(): lax.all_to_all(shares, ALL, split_axis=0, concat_axis=0, tiled=True)  7.3 us
    all_to_all x1, waiting for transfers between devices, direct(): lax.all_to_all(shares, ALL, split_axis=0, concat_axis=0, tiled=True)  7.01 us
    pallas_call x1, Pallas kernels, direct(): pl.pallas_call(functools.partial(share_kernel, length), out_shape=jax.Sha...  1.86 us
    pallas_call x1, Pallas kernels, direct(): pl.pallas_call(weights_kernel, out_shape=[jax.ShapeDtypeStruct((rows * ch...  1.53 us
    pallas_call x1, Pallas kernels, direct(): pl.pallas_call(layers_kernel, out_shape=jax.ShapeDtypeStruct((channels, T...  1.52 us
  transfers between devices with their start and end apart: 1, of which 1 were waited for; matrix products, arithmetic and copies ran while one was open for 0% of the time, Pallas kernels for 8%

profile of v5, /device:TPU:0, one launch (start us, length us, event | category | flops | bytes accessed | tf_op | source)
XLA Modules:
  0.0 19.3 jit_solution(6767819313101895697)
XLA Ops:
  0.0 1.9 %shares.1 = bf16[32,24,128]{2,1,0:T(8,128)(2,1)} custom-call(s32[1,1,2]{2,1,0:T(1,128)} %cover_in.1, bf16[1,2,128,256]{3,2,1,0:T(8,128)(2,1)} %parts_in.1), custom_call_target="tpu_custom_call" | custom-call | tf_op jit(solution)/shard_map/shares/pallas_call | solution.py:370
  1.9 7.3 %all-to-all-start = ((bf16[32,24,128]{2,1,0:T(8,128)(2,1)}), bf16[32,24,128]{2,1,0:T(8,128)(2,1)S(1)}, u32[]{:S(2)}, u32[]{:S(2)}) async-start(bf16[32,24,128]{2,1,0:T(8,128)(2,1)} %shares.1), calls=%async_computation | async-start | bytes 393216 | tf_op jit(solution)/shard_map/all_to_all | solution.py:384
  9.2 1.5 %weights.1 = (bf16[320,144]{1,0:T(8,128)(2,1)S(1)}, bf16[256,960]{1,0:T(8,128)(2,1)S(1)}, f32[256,128]{1,0:T(8,128)S(1)}, bf16[1024,256]{1,0:T(8,128)(2,1)S(1)}) custom-call(f32[3,3,32]{2,1,0:T(4,128)} %bitcast.3, f32[1,32]{1,0:T(1,128)} %bitcast.4, bf16[3,3,32,32]{3,2,1,0:T(8,128)(2,1)} %two_in.1, f32[1,32]{1,0:T(1,128)} %bitcast.5, ...), custom_call_target="tpu_custom_call" | custom-call | tf_op jit(solution)/shard_map/weights/pallas_call | solution.py:386
  10.7 7.0 %all-to-all-done.shares = bf16[32,24,128]{2,1,0:T(8,128)(2,1)S(1)} async-done(((bf16[32,24,128]{2,1,0:T(8,128)(2,1)}), bf16[32,24,128]{2,1,0:T(8,128)(2,1)S(1)}, u32[]{:S(2)}, u32[]{:S(2)}) %all-to-all-start) | async-done | bytes 196640 | tf_op jit(solution)/shard_map/all_to_all | solution.py:384
  17.7 1.5 %layers.1 = bf16[32,8,256]{2,1,0:T(8,128)(2,1)} custom-call(bf16[32,24,128]{2,1,0:T(8,128)(2,1)S(1)} %all-to-all-done.shares, bf16[320,144]{1,0:T(8,128)(2,1)S(1)} %get-tuple-element.9.weights_one, bf16[256,960]{1,0:T(8,128)(2,1)S(1)} %get-tuple-element.10.weights_two, f32[256,128]{1,0:T(8,128)S(1)} %get-tuple-element.11.bias_rows, ...), custom_call_target="tpu_custom_call" | custom-call | tf_op jit(solution)/shard_map/layers/pallas_call | solution.py:406
Async XLA Ops:
  1.9 15.9 %all-to-all-start = ((bf16[32,24,128]{2,1,0:T(8,128)(2,1)}), bf16[32,24,128]{2,1,0:T(8,128)(2,1)S(1)}, u32[]{:S(2)}, u32[]{:S(2)}) async-start(bf16[32,24,128]{2,1,0:T(8,128)(2,1)} %shares.1), calls=%async_computation | async-start | bytes 393216 | tf_op jit(solution)/shard_map/all_to_all | solution.py:384

commit v6 on v5

--- a/solution.py
+++ b/solution.py
@@ -172,15 +172,20 @@
 def make_first(first, length):
     tall, cols = first.shape[0] // 2, first.shape[1]
     image_len = tall - TILE
-    blocks = -(-tall // (TILE * TILE)) * TILE
     start = lax.axis_index("col") * cols - length // 2
-    row = lax.broadcasted_iota(jnp.int32, (blocks, cols), 0) * TILE - HALO - image_len // 2
-    cos_far, sin_far = phases(row * (start + lax.broadcasted_iota(jnp.int32, (blocks, cols), 1)), length)
+    place = start + lax.broadcasted_iota(jnp.int32, (TILE, cols), 1)
     row = lax.broadcasted_iota(jnp.int32, (TILE, cols), 0)
-    cos_near, sin_near = phases(row * (start + lax.broadcasted_iota(jnp.int32, (TILE, cols), 1)), length)
+    cos_far, sin_far = phases((row * TILE * TILE - HALO - image_len // 2) * place, length)
+    cos_mid, sin_mid = phases(row * TILE * place, length)
+    cos_near, sin_near = phases(row * place, length)
     cosines, sines = [], []
     for k in range(tall // TILE):
-        cos_at, sin_at = cos_far[k : k + 1], sin_far[k : k + 1]
+        n, m = divmod(k, TILE)
+        if m == 0:
+            cos_at, sin_at = cos_far[n : n + 1], sin_far[n : n + 1]
+            cos_tile = cos_at * cos_mid - sin_at * sin_mid
+            sin_tile = sin_at * cos_mid + cos_at * sin_mid
+        cos_at, sin_at = cos_tile[m : m + 1], sin_tile[m : m + 1]
         cos = cos_at * cos_near - sin_at * sin_near
         sin = sin_at * cos_near + cos_at * sin_near
         pixel = row + (TILE * k - HALO)

time: 19.5 us -> 19.5 us (level)
  no operation moved by 1% of the time
where the time goes in v6:
time: 19.5 us; the launch traced here: 19.3 us
  starting transfers between devices  7.3 us (37%)
  waiting for transfers between devices  7.01 us (36%)
  Pallas kernels  4.92 us (25%)
    all_to_all x1, starting transfers between devices, direct(): lax.all_to_all(shares, ALL, split_axis=0, concat_axis=0, tiled=True)  7.3 us
    all_to_all x1, waiting for transfers between devices, direct(): lax.all_to_all(shares, ALL, split_axis=0, concat_axis=0, tiled=True)  7.01 us
    pallas_call x1, Pallas kernels, direct(): pl.pallas_call(functools.partial(share_kernel, length), out_shape=jax.Sha...  1.86 us
    pallas_call x1, Pallas kernels, direct(): pl.pallas_call(weights_kernel, out_shape=[jax.ShapeDtypeStruct((rows * ch...  1.53 us
    pallas_call x1, Pallas kernels, direct(): pl.pallas_call(layers_kernel, out_shape=jax.ShapeDtypeStruct((channels, T...  1.52 us
  transfers between devices with their start and end apart: 1, of which 1 were waited for; matrix products, arithmetic and copies ran while one was open for 0% of the time, Pallas kernels for 8%

profile of v6, /device:TPU:0, one launch (start us, length us, event | category | flops | bytes accessed | tf_op | source)
XLA Modules:
  0.0 19.3 jit_solution(15954506334478039674)
XLA Ops:
  0.0 1.9 %shares.1 = bf16[32,24,128]{2,1,0:T(8,128)(2,1)} custom-call(s32[1,1,2]{2,1,0:T(1,128)} %cover_in.1, bf16[1,2,128,256]{3,2,1,0:T(8,128)(2,1)} %parts_in.1), custom_call_target="tpu_custom_call" | custom-call | tf_op jit(solution)/shard_map/shares/pallas_call | solution.py:375
  1.9 7.3 %all-to-all-start = ((bf16[32,24,128]{2,1,0:T(8,128)(2,1)}), bf16[32,24,128]{2,1,0:T(8,128)(2,1)S(1)}, u32[]{:S(2)}, u32[]{:S(2)}) async-start(bf16[32,24,128]{2,1,0:T(8,128)(2,1)} %shares.1), calls=%async_computation | async-start | bytes 393216 | tf_op jit(solution)/shard_map/all_to_all | solution.py:389
  9.2 1.5 %weights.1 = (bf16[320,144]{1,0:T(8,128)(2,1)S(1)}, bf16[256,960]{1,0:T(8,128)(2,1)S(1)}, f32[256,128]{1,0:T(8,128)S(1)}, bf16[1024,256]{1,0:T(8,128)(2,1)S(1)}) custom-call(f32[3,3,32]{2,1,0:T(4,128)} %bitcast.3, f32[1,32]{1,0:T(1,128)} %bitcast.4, bf16[3,3,32,32]{3,2,1,0:T(8,128)(2,1)} %two_in.1, f32[1,32]{1,0:T(1,128)} %bitcast.5, ...), custom_call_target="tpu_custom_call" | custom-call | tf_op jit(solution)/shard_map/weights/pallas_call | solution.py:391
  10.7 7.0 %all-to-all-done.shares = bf16[32,24,128]{2,1,0:T(8,128)(2,1)S(1)} async-done(((bf16[32,24,128]{2,1,0:T(8,128)(2,1)}), bf16[32,24,128]{2,1,0:T(8,128)(2,1)S(1)}, u32[]{:S(2)}, u32[]{:S(2)}) %all-to-all-start) | async-done | bytes 196640 | tf_op jit(solution)/shard_map/all_to_all | solution.py:389
  17.7 1.5 %layers.1 = bf16[32,8,256]{2,1,0:T(8,128)(2,1)} custom-call(bf16[32,24,128]{2,1,0:T(8,128)(2,1)S(1)} %all-to-all-done.shares, bf16[320,144]{1,0:T(8,128)(2,1)S(1)} %get-tuple-element.9.weights_one, bf16[256,960]{1,0:T(8,128)(2,1)S(1)} %get-tuple-element.10.weights_two, f32[256,128]{1,0:T(8,128)S(1)} %get-tuple-element.11.bias_rows, ...), custom_call_target="tpu_custom_call" | custom-call | tf_op jit(solution)/shard_map/layers/pallas_call | solution.py:411
Async XLA Ops:
  1.9 15.9 %all-to-all-start = ((bf16[32,24,128]{2,1,0:T(8,128)(2,1)}), bf16[32,24,128]{2,1,0:T(8,128)(2,1)S(1)}, u32[]{:S(2)}, u32[]{:S(2)}) async-start(bf16[32,24,128]{2,1,0:T(8,128)(2,1)} %shares.1), calls=%async_computation | async-start | bytes 393216 | tf_op jit(solution)/shard_map/all_to_all | solution.py:389
